TPU v7x, 256 devices: a whole 4x4x8 slice. The times are simulated.
256 devices in a mesh: gx: 32 (over z, x), gy: 8 (over y, core).
Axes of the slice: x: 4, y: 4, z: 8, core: 2. Of those that a mesh axis runs over, the one named last changes fastest.
Arguments:
- phase_label: int32 [512, 256, 128], P('gx', 'gy'), may hold values from 0 to 2
- tab_index: int32 [512, 256, 128], P('gx', 'gy'), may hold values from 0 to 63
- source_field: float32 [512, 256, 128], P('gx', 'gy'), may hold values from -8 to 8
- sigma_table: float32 [3], replicated, may hold values from 0.2 to 5
- pattern_gain: float32 [16, 64], replicated, may hold values from -6 to 6
Outputs:
- solution: float32 [16, 512, 256, 128], P(None, 'gx', 'gy')
- residual: float32 [16, 512, 256, 128], P(None, 'gx', 'gy')
All inputs are finite; a program needn't handle non-finite values.
Results may differ from a plain program's by a relative error of at most 0.0003.
Values sent between devices are 32-bit elements; how exact they have to be, the bound alone decides.
A program may use at most 192 MiB of HBM per device.

v0:
```python
import jax
import jax.numpy as jnp
import numpy as np
from jax import lax
from jax.sharding import PartitionSpec as P

S = 4
NRHS = 16
TABS = 64
OFFSETS = ((-1, 0, 0), (1, 0, 0), (0, -1, 0), (0, 1, 0), (0, 0, -1), (0, 0, 1))


def with_halo(value, sides, width):
    for axis, dim in sides:
        size, length = (lax.axis_size(axis), value.shape[dim])
        up = [(i, (i + 1) % size) for i in range(size - 1)]
        down = [(j, i) for i, j in up]
        last = lax.slice_in_dim(value, length - width, length, axis=dim)
        initial = lax.slice_in_dim(value, 0, width, axis=dim)
        before = lax.ppermute(last, axis, up)
        after = lax.ppermute(initial, axis, down)
        value = jnp.concatenate([before, value, after], axis=dim)
    return value


def moved(array, a, b, c):
    sx = array.shape[-3]
    sy = array.shape[-2]
    sz = array.shape[-1]
    return array[..., 1 + a : sx - 1 + a, 1 + b : sy - 1 + b, 1 + c : sz - 1 + c]


def neighbour_mean(fields, conduct):
    fields_z = jnp.pad(fields, ((0, 0), (0, 0), (0, 0), (1, 1)))
    conduct_z = jnp.pad(conduct, ((0, 0), (0, 0), (1, 1)))
    centre = moved(conduct_z, 0, 0, 0)
    summed = jnp.zeros(fields.shape[:1] + centre.shape, jnp.float32)
    weights = jnp.zeros(centre.shape, jnp.float32)
    for offset in OFFSETS:
        face = 0.5 * (centre + moved(conduct_z, offset[0], offset[1], offset[2]))
        summed = summed + face[None] * moved(fields_z, offset[0], offset[1], offset[2])
        weights = weights + face
    inside = centre > 0
    return jnp.where(inside[None], summed / jnp.where(inside, weights, 1.0)[None], 0.0)


def difference_matrix():
    matrix = np.zeros((NRHS * (S + 1), NRHS * S), np.float32)
    for step in range(S):
        for column in range(NRHS):
            matrix[step * NRHS + column, step * NRHS + column] = 1.0
            matrix[(step + 1) * NRHS + column, step * NRHS + column] = -1.0
    return jnp.asarray(matrix)


def least_squares(gram):
    highest = lax.Precision.HIGHEST
    diff = difference_matrix()
    hess = jnp.dot(diff.T, jnp.dot(gram, diff, precision=highest), precision=highest)
    right_block = jnp.dot(diff.T, gram[:, :NRHS], precision=highest)
    factor = jnp.linalg.cholesky(hess)
    coeffs = jax.scipy.linalg.cho_solve((factor, True), right_block)
    return (diff, coeffs)


def shards(phase_label, tab_index, source_field, sigma_table, pattern_gain):
    highest = lax.Precision.HIGHEST
    shape = phase_label.shape
    conduct = jnp.where(
        phase_label == 0,
        sigma_table[0],
        jnp.where(phase_label == 1, sigma_table[1], sigma_table[2]),
    )
    onehot = (tab_index.reshape(1, -1) == jnp.arange(TABS, dtype=jnp.int32)[:, None]).astype(
        jnp.float32
    )
    start = jnp.dot(pattern_gain, onehot, precision=highest) * source_field.reshape(1, -1)
    start = start.reshape((NRHS,) + shape)
    stacked = jnp.concatenate([conduct[None], start], 0)
    krylov = [start]
    ghosted = with_halo(stacked, (("gx", 1), ("gy", 2)), 1)
    conduct_wide = ghosted[0]
    current = neighbour_mean(ghosted[1:], conduct_wide)
    krylov.append(current)
    for step in range(S - 1):
        padded = with_halo(current, (("gx", 1), ("gy", 2)), 1)
        current = neighbour_mean(padded, conduct_wide)
        krylov.append(current)
    flat = jnp.concatenate([field.reshape(NRHS, -1) for field in krylov], 0)
    gram = lax.psum(jnp.dot(flat, flat.T, precision=highest), ("gx", "gy"))
    diff, coeffs = least_squares(gram)
    solution = jnp.dot(coeffs.T, flat[: S * NRHS], precision=highest)
    combined = jnp.dot(diff, coeffs, precision=highest)
    residual = flat[:NRHS] - jnp.dot(combined.T, flat, precision=highest)
    return (solution.reshape((NRHS,) + shape), residual.reshape((NRHS,) + shape))


def solution(mesh):
    placed = (P("gx", "gy", None), P("gx", "gy", None), P("gx", "gy", None), P(), P())
    return jax.shard_map(
        shards,
        mesh=mesh,
        in_specs=placed,
        out_specs=(P(None, "gx", "gy", None), P(None, "gx", "gy", None)),
        check_vma=False,
    )
```

profile of v0, /device:TPU:1, one launch (start us, length us, event | category | flops | bytes accessed | tf_op | source)
XLA Modules:
  0.0 357.0 jit_solution(16355060055221915815)
XLA Ops:
  2.1 7.5 %constant_dynamic-update-slice_fusion.3 = (f32[80,65536]{1,0:T(8,128)}, f32[65536,16]{0,1:T(8,128)S(1)}) fusion(f32[65536]{0:T(1024)} %bitcast.93, f32[16,64]{1,0:T(8,128)S(1)} %copy-done, s32[65536]{0:T(1024)} %bitcast.94), kind=kOutput, calls=%fused_computation.175 | convolution fusion | flops 810549248 | bytes 8916992 | tf_op jit(solution)/shard_map/dot_general | solution.py:77
  26.9 5.0 %collective-permute-start.2 = (f32[17,18,1,128]{3,2,1,0:T(1,128)S(1)}, f32[17,18,1,128]{3,2,1,0:T(1,128)S(1)}, u32[]{:S(2)}, u32[]{:S(2)}) collective-permute-start(f32[17,18,1,128]{3,2,1,0:T(1,128)S(1)} %get-tuple-element.10), channel_id=1, source_target_pairs={{0,1},{1,2},{2,3},{3,4},{4,5},{5,6},{6,7},{8,9},{9,10},{10,11},{11... | collective-permute-start | bytes 470024 | tf_op jit(solution)/shard_map/ppermute | solution.py:20
  39.7 9.6 %select_maximum_fusion.12 = f32[16,18,34,130]{3,2,1,0:T(8,128)} fusion(f32[17,18,1,128]{3,2,1,0:T(1,128)S(1)} %collective-permute-done.3, f32[17,18,1,128]{3,2,1,0:T(1,128)S(1)} %collective-permute-done.2, f32[17,1,32,128]{3,2,1,0:T(8,128)S(1)} %collective-permute-done.1, f32[17,1,32,128]{3,2,1,0:T(8,128)S(1)} %collective-permute-done, ...), kind=kLoop, calls=%fused_computation.25 | loop fusion | flops 17821440 | bytes 10418688 | tf_op jit(solution)/shard_map/concatenate | solution.py:22
  49.3 9.0 %fusion.45 = f32[16,16,32,128]{3,2,1,0:T(8,128)S(1)} fusion(f32[16,18,34,130]{3,2,1,0:T(8,128)} %select_maximum_fusion.12, f32[17,18,1,128]{3,2,1,0:T(1,128)} %copy-done.13, f32[17,1,32,128]{3,2,1,0:T(8,128)} %copy-done.9, f32[17,1,32,128]{3,2,1,0:T(8,128)} %copy-done.8, f32[16,16,32,128]{3,2,1,0:T(8,128)S(1)} %bitcast.84, ...), kind=kLoop, calls=%fused_computation.102 | loop fusion | flops 26214400 | bytes 19810304 | tf_op jit(solution)/shard_map/jit(_where)/select_n | solution.py:44
  69.1 5.2 %collective-permute-start.6 = (f32[16,18,1,128]{3,2,1,0:T(1,128)S(1)}, f32[16,18,1,128]{3,2,1,0:T(1,128)S(1)}, u32[]{:S(2)}, u32[]{:S(2)}) collective-permute-start(f32[16,18,1,128]{3,2,1,0:T(1,128)S(1)} %get-tuple-element.16), channel_id=1, source_target_pairs={{0,1},{1,2},{2,3},{3,4},{4,5},{5,6},{6,7},{8,9},{9,10},{10,11},{11... | collective-permute-start | bytes 442376 | tf_op jit(solution)/shard_map/ppermute | solution.py:20
  80.9 8.9 %select_maximum_fusion.8 = f32[16,18,34,130]{3,2,1,0:T(8,128)} fusion(f32[16,18,1,128]{3,2,1,0:T(1,128)S(1)} %collective-permute-done.7, f32[16,18,1,128]{3,2,1,0:T(1,128)S(1)} %collective-permute-done.6, f32[16,1,32,128]{3,2,1,0:T(8,128)S(1)} %collective-permute-done.5, f32[16,16,32,128]{3,2,1,0:T(8,128)S(1)} %fusion.45, ...), kind=kLoop, calls=%fused_computation.21 | loop fusion | flops 15275520 | bytes 10105344 | tf_op jit(solution)/shard_map/concatenate | solution.py:22
  89.8 10.9 %fusion.34 = f32[16,16,32,128]{3,2,1,0:T(8,128)S(1)} fusion(f32[16,18,34,130]{3,2,1,0:T(8,128)} %select_maximum_fusion.8, f32[16,18,1,128]{3,2,1,0:T(1,128)S(1)} %collective-permute-done.7, f32[16,1,32,128]{3,2,1,0:T(8,128)S(1)} %collective-permute-done.5, f32[16,16,32,128]{3,2,1,0:T(8,128)S(1)} %fusion.45, ...), kind=kLoop, calls=%fused_computation.81 | loop fusion | flops 22020096 | bytes 19496960 | tf_op jit(solution)/shard_map/jit(_where)/select_n | solution.py:44
  100.7 4.4 %collective-permute-start.8 = (f32[16,1,32,128]{3,2,1,0:T(8,128)S(1)}, f32[16,1,32,128]{3,2,1,0:T(8,128)S(1)}, u32[]{:S(2)}, u32[]{:S(2)}) collective-permute-start(f32[16,1,32,128]{3,2,1,0:T(8,128)S(1)} %get-tuple-element.22), channel_id=1, source_target_pairs={{0,8},{8,16},{16,24},{24,32},{32,40},{40,48},{48,56},{56,64},{64,7... | collective-permute-start | bytes 786440 | tf_op jit(solution)/shard_map/ppermute | solution.py:20
  108.5 4.4 %collective-permute-done.9 = f32[16,1,32,128]{3,2,1,0:T(8,128)S(1)} collective-permute-done((f32[16,1,32,128]{3,2,1,0:T(8,128)S(1)}, f32[16,1,32,128]{3,2,1,0:T(8,128)S(1)}, u32[]{:S(2)}, u32[]{:S(2)}) %collective-permute-start.9) | collective-permute-done | bytes 262176 | tf_op jit(solution)/shard_map/ppermute | solution.py:21
  113.2 4.5 %collective-permute-start.10 = (f32[16,18,1,128]{3,2,1,0:T(1,128)S(1)}, f32[16,18,1,128]{3,2,1,0:T(1,128)S(1)}, u32[]{:S(2)}, u32[]{:S(2)}) collective-permute-start(f32[16,18,1,128]{3,2,1,0:T(1,128)S(1)} %get-tuple-element.14), channel_id=1, source_target_pairs={{0,1},{1,2},{2,3},{3,4},{4,5},{5,6},{6,7},{8,9},{9,10},{10,11},{11... | collective-permute-start | bytes 442376 | tf_op jit(solution)/shard_map/ppermute | solution.py:20
  119.8 4.5 %constant_dynamic-update-slice_fusion.2 = f32[80,65536]{1,0:T(8,128)} fusion(f32[80,65536]{1,0:T(8,128)} %get-tuple-element.29, f32[2,8,512,128]{3,2,1,0:T(8,128)S(1)} %bitcast.74), kind=kLoop, calls=%fused_computation.174 | loop fusion | bytes 8388608
  130.0 8.9 %select_maximum_fusion.4 = f32[16,18,34,130]{3,2,1,0:T(8,128)} fusion(f32[16,18,1,128]{3,2,1,0:T(1,128)S(1)} %collective-permute-done.11, f32[16,18,1,128]{3,2,1,0:T(1,128)S(1)} %collective-permute-done.10, f32[16,1,32,128]{3,2,1,0:T(8,128)S(1)} %collective-permute-done.9, f32[16,16,32,128]{3,2,1,0:T(8,128)S(1)} %fusion.34, ...), kind=kLoop, calls=%fused_computation.17 | loop fusion | flops 15275520 | bytes 10105344 | tf_op jit(solution)/shard_map/concatenate | solution.py:22
  138.8 8.1 %fusion.23 = f32[16,16,32,128]{3,2,1,0:T(8,128)S(1)} fusion(f32[16,18,34,130]{3,2,1,0:T(8,128)} %select_maximum_fusion.4, f32[16,18,1,128]{3,2,1,0:T(1,128)} %copy-done.16, f32[16,1,32,128]{3,2,1,0:T(8,128)} %copy-done.11, f32[16,16,32,128]{3,2,1,0:T(8,128)S(1)} %fusion.34, f32[16,1,32,128]{3,2,1,0:T(8,128)} %copy-done.10, f32[16,18,1,128]{3,2,1,0:T(1,128)} %copy-done.15, ...), kind=kLoop, calls=%fused_computation.60 | loop fusion | flops 22020096 | bytes 19496960 | tf_op jit(solution)/shard_map/jit(_where)/select_n | solution.py:44
  152.5 4.4 %constant_dynamic-update-slice_fusion.1 = f32[80,65536]{1,0:T(8,128)} fusion(f32[80,65536]{1,0:T(8,128)} %constant_dynamic-update-slice_fusion.2, f32[2,8,512,128]{3,2,1,0:T(8,128)S(1)} %bitcast.76), kind=kLoop, calls=%fused_computation.173 | loop fusion | bytes 8388608
  171.8 4.4 %copy.26 = f32[2,8,512,128]{3,1,2,0:T(8,128)} copy(f32[2,8,512,128]{3,2,1,0:T(8,128)S(1)} %bitcast.79) | data formatting | bytes 8388608
  176.2 9.0 %select_maximum_fusion = f32[16,18,34,130]{3,2,1,0:T(8,128)} fusion(f32[16,18,1,128]{3,2,1,0:T(1,128)S(1)} %collective-permute-done.15, f32[16,18,1,128]{3,2,1,0:T(1,128)S(1)} %collective-permute-done.14, f32[16,1,32,128]{3,2,1,0:T(8,128)S(1)} %collective-permute-done.13, f32[16,16,32,128]{3,2,1,0:T(8,128)S(1)} %fusion.23, ...), kind=kLoop, calls=%fused_computation.13 | loop fusion | flops 15275520 | bytes 10105344 | tf_op jit(solution)/shard_map/concatenate | solution.py:22
  185.2 10.9 %fusion.12 = f32[16,16,32,128]{3,2,1,0:T(8,128)S(1)} fusion(f32[16,18,34,130]{3,2,1,0:T(8,128)} %select_maximum_fusion, f32[16,18,1,128]{3,2,1,0:T(1,128)S(1)} %collective-permute-done.15, f32[16,1,32,128]{3,2,1,0:T(8,128)S(1)} %collective-permute-done.13, f32[16,16,32,128]{3,2,1,0:T(8,128)S(1)} %fusion.23, ...), kind=kLoop, calls=%fused_computation.39 | loop fusion | flops 22020096 | bytes 19496960 | tf_op jit(solution)/shard_map/jit(_where)/select_n | solution.py:44
  200.5 23.0 %fusion.85 = f32[80,80]{1,0:T(8,128)S(1)} fusion(f32[80,65536]{1,0:T(8,128)} %bitcast_dynamic-update-slice_fusion), kind=kOutput, calls=%fused_computation.182 | convolution fusion | flops 5033164800 | bytes 20997120 | tf_op jit(solution)/shard_map/dot_general | solution.py:90
  223.5 85.6 %psum.7 = f32[80,80]{1,0:T(8,128)S(1)} all-reduce(f32[80,80]{1,0:T(8,128)S(1)} %fusion.85), channel_id=1, replica_groups=mesh['gx'=32,'gy'=8] {'gx','gy'}, use_global_device_ids=true, to_apply=%region_0.1 | all-reduce | flops 6400 | bytes 51200 | tf_op jit(solution)/shard_map/psum | solution.py:90
  309.9 5.8 %cholesky.16 = f32[64,64]{1,0:T(8,128)S(1)} custom-call(f32[64,64]{1,0:T(8,128)S(1)} %fusion.73), custom_call_target="Cholesky" | custom-call | tf_op jit(solution)/shard_map/jit(cholesky)/cholesky | solution.py:61
  317.1 4.9 %custom-call.10 = f32[1,64,64]{1,2,0:T(8,128)S(1)} custom-call(f32[1,64,64]{2,1,0:T(8,128)S(1)} %fusion.68), custom_call_target="InvertDiagBlocksLowerTriangular" | custom-call | tf_op jit(solution)/shard_map/jit(_cho_solve)/triangular_solve | solution.py:62
  322.6 13.5 %fusion.57 = f32[2,8,512,128]{3,1,2,0:T(8,128)S(1)} fusion(f32[16,80]{1,0:T(8,128)S(1)} %fusion.88, f32[80,65536]{1,0:T(8,128)} %bitcast_dynamic-update-slice_fusion, f32[65536,16]{0,1:T(8,128)} %copy-done.2), kind=kOutput, calls=%fused_computation.125 | convolution fusion | flops 1007681536 | bytes 29365248 | tf_op jit(solution)/shard_map/dot_general | solution.py:94
  338.9 12.9 %fusion.54 = f32[2,8,512,128]{3,1,2,0:T(8,128)} fusion(f32[64,16]{0,1:T(8,128)S(1)} %fusion.69, f32[16,65536]{1,0:T(8,128)} %bitcast.90, f32[16,65536]{1,0:T(8,128)} %bitcast.89, f32[16,65536]{1,0:T(8,128)} %bitcast.88, f32[16,65536]{1,0:T(8,128)} %bitcast.86), kind=kOutput, calls=%fused_computation.124 | convolution fusion | flops 817889280 | bytes 20975616 | tf_op jit(solution)/shard_map/dot_general | solution.py:92
  351.8 5.0 %copy.14 = f32[2,8,512,128]{3,2,1,0:T(8,128)} copy(f32[2,8,512,128]{3,1,2,0:T(8,128)} %fusion.54) | data formatting | bytes 8388608
  (92 shorter events, 85.4 us)
Async XLA Ops:
  13.6 9.3 %collective-permute-start = (f32[17,1,32,128]{3,2,1,0:T(8,128)S(1)}, f32[17,1,32,128]{3,2,1,0:T(8,128)S(1)}, u32[]{:S(2)}, u32[]{:S(2)}) collective-permute-start(f32[17,1,32,128]{3,2,1,0:T(8,128)S(1)} %get-tuple-element.18), channel_id=1, source_target_pairs={{0,8},{8,16},{16,24},{24,32},{32,40},{40,48},{48,56},{56,64},{64,7... | collective-permute-start | bytes 835592 | tf_op jit(solution)/shard_map/ppermute | solution.py:20
  17.6 9.1 %collective-permute-start.1 = (f32[17,1,32,128]{3,2,1,0:T(8,128)S(1)}, f32[17,1,32,128]{3,2,1,0:T(8,128)S(1)}, u32[]{:S(2)}, u32[]{:S(2)}) collective-permute-start(f32[17,1,32,128]{3,2,1,0:T(8,128)S(1)} %get-tuple-element.19), channel_id=1, source_target_pairs={{8,0},{16,8},{24,16},{32,24},{40,32},{48,40},{56,48},{64,56},{72,6... | collective-permute-start | bytes 835592 | tf_op jit(solution)/shard_map/ppermute | solution.py:21
  22.9 16.8 %copy-start.8 = (f32[17,1,32,128]{3,2,1,0:T(8,128)}, f32[17,1,32,128]{3,2,1,0:T(8,128)S(1)}, u32[]{:S(2)}) copy-start(f32[17,1,32,128]{3,2,1,0:T(8,128)S(1)} %collective-permute-done) | copy-start | bytes 835588
  26.9 7.1 %collective-permute-start.2 = (f32[17,18,1,128]{3,2,1,0:T(1,128)S(1)}, f32[17,18,1,128]{3,2,1,0:T(1,128)S(1)}, u32[]{:S(2)}, u32[]{:S(2)}) collective-permute-start(f32[17,18,1,128]{3,2,1,0:T(1,128)S(1)} %get-tuple-element.10), channel_id=1, source_target_pairs={{0,1},{1,2},{2,3},{3,4},{4,5},{5,6},{6,7},{8,9},{9,10},{10,11},{11... | collective-permute-start | bytes 470024 | tf_op jit(solution)/shard_map/ppermute | solution.py:20
  31.9 6.6 %collective-permute-start.3 = (f32[17,18,1,128]{3,2,1,0:T(1,128)S(1)}, f32[17,18,1,128]{3,2,1,0:T(1,128)S(1)}, u32[]{:S(2)}, u32[]{:S(2)}) collective-permute-start(f32[17,18,1,128]{3,2,1,0:T(1,128)S(1)} %get-tuple-element.11), channel_id=1, source_target_pairs={{1,0},{2,1},{3,2},{4,3},{5,4},{6,5},{7,6},{9,8},{10,9},{11,10},{12... | collective-permute-start | bytes 470024 | tf_op jit(solution)/shard_map/ppermute | solution.py:21
  58.4 6.4 %collective-permute-start.4 = (f32[16,1,32,128]{3,2,1,0:T(8,128)S(1)}, f32[16,1,32,128]{3,2,1,0:T(8,128)S(1)}, u32[]{:S(2)}, u32[]{:S(2)}) collective-permute-start(f32[16,1,32,128]{3,2,1,0:T(8,128)S(1)} %get-tuple-element.24), channel_id=1, source_target_pairs={{0,8},{8,16},{16,24},{24,32},{32,40},{40,48},{48,56},{56,64},{64,7... | collective-permute-start | bytes 786440 | tf_op jit(solution)/shard_map/ppermute | solution.py:20
  61.5 7.4 %collective-permute-start.5 = (f32[16,1,32,128]{3,2,1,0:T(8,128)S(1)}, f32[16,1,32,128]{3,2,1,0:T(8,128)S(1)}, u32[]{:S(2)}, u32[]{:S(2)}) collective-permute-start(f32[16,1,32,128]{3,2,1,0:T(8,128)S(1)} %get-tuple-element.25), channel_id=1, source_target_pairs={{8,0},{16,8},{24,16},{32,24},{40,32},{48,40},{56,48},{64,56},{72,6... | collective-permute-start | bytes 786440 | tf_op jit(solution)/shard_map/ppermute | solution.py:21
  69.1 7.4 %collective-permute-start.6 = (f32[16,18,1,128]{3,2,1,0:T(1,128)S(1)}, f32[16,18,1,128]{3,2,1,0:T(1,128)S(1)}, u32[]{:S(2)}, u32[]{:S(2)}) collective-permute-start(f32[16,18,1,128]{3,2,1,0:T(1,128)S(1)} %get-tuple-element.16), channel_id=1, source_target_pairs={{0,1},{1,2},{2,3},{3,4},{4,5},{5,6},{6,7},{8,9},{9,10},{10,11},{11... | collective-permute-start | bytes 442376 | tf_op jit(solution)/shard_map/ppermute | solution.py:20
  74.3 15.5 %copy-start.3 = (f32[16,32,128]{2,1,0:T(8,128)S(1)}, f32[16,32,128]{2,1,0:T(8,128)}, u32[]{:S(2)}) copy-start(f32[16,32,128]{2,1,0:T(8,128)} %get-tuple-element.6) | copy-start | bytes 786436
  74.3 15.5 %copy-start.4 = (f32[16,32,128]{2,1,0:T(8,128)S(1)}, f32[16,32,128]{2,1,0:T(8,128)}, u32[]{:S(2)}) copy-start(f32[16,32,128]{2,1,0:T(8,128)} %get-tuple-element.7) | copy-start | bytes 786436
  74.3 15.5 %copy-start.6 = (f32[16,32,128]{2,1,0:T(8,128)S(1)}, f32[16,32,128]{2,1,0:T(8,128)}, u32[]{:S(2)}) copy-start(f32[16,32,128]{2,1,0:T(8,128)} %get-tuple-element.8) | copy-start | bytes 786436
  74.3 6.6 %collective-permute-start.7 = (f32[16,18,1,128]{3,2,1,0:T(1,128)S(1)}, f32[16,18,1,128]{3,2,1,0:T(1,128)S(1)}, u32[]{:S(2)}, u32[]{:S(2)}) collective-permute-start(f32[16,18,1,128]{3,2,1,0:T(1,128)S(1)} %get-tuple-element.17), channel_id=1, source_target_pairs={{1,0},{2,1},{3,2},{4,3},{5,4},{6,5},{7,6},{9,8},{10,9},{11,10},{12... | collective-permute-start | bytes 442376 | tf_op jit(solution)/shard_map/ppermute | solution.py:21
  100.7 7.8 %collective-permute-start.8 = (f32[16,1,32,128]{3,2,1,0:T(8,128)S(1)}, f32[16,1,32,128]{3,2,1,0:T(8,128)S(1)}, u32[]{:S(2)}, u32[]{:S(2)}) collective-permute-start(f32[16,1,32,128]{3,2,1,0:T(8,128)S(1)} %get-tuple-element.22), channel_id=1, source_target_pairs={{0,8},{8,16},{16,24},{24,32},{32,40},{40,48},{48,56},{56,64},{64,7... | collective-permute-start | bytes 786440 | tf_op jit(solution)/shard_map/ppermute | solution.py:20
  105.2 7.8 %collective-permute-start.9 = (f32[16,1,32,128]{3,2,1,0:T(8,128)S(1)}, f32[16,1,32,128]{3,2,1,0:T(8,128)S(1)}, u32[]{:S(2)}, u32[]{:S(2)}) collective-permute-start(f32[16,1,32,128]{3,2,1,0:T(8,128)S(1)} %get-tuple-element.23), channel_id=1, source_target_pairs={{8,0},{16,8},{24,16},{32,24},{40,32},{48,40},{56,48},{64,56},{72,6... | collective-permute-start | bytes 786440 | tf_op jit(solution)/shard_map/ppermute | solution.py:21
  108.5 20.2 %copy-start.10 = (f32[16,1,32,128]{3,2,1,0:T(8,128)}, f32[16,1,32,128]{3,2,1,0:T(8,128)S(1)}, u32[]{:S(2)}) copy-start(f32[16,1,32,128]{3,2,1,0:T(8,128)S(1)} %collective-permute-done.8) | copy-start | bytes 786436
  113.0 15.7 %copy-start.11 = (f32[16,1,32,128]{3,2,1,0:T(8,128)}, f32[16,1,32,128]{3,2,1,0:T(8,128)S(1)}, u32[]{:S(2)}) copy-start(f32[16,1,32,128]{3,2,1,0:T(8,128)S(1)} %collective-permute-done.9) | copy-start | bytes 786436
  113.2 15.5 %collective-permute-start.10 = (f32[16,18,1,128]{3,2,1,0:T(1,128)S(1)}, f32[16,18,1,128]{3,2,1,0:T(1,128)S(1)}, u32[]{:S(2)}, u32[]{:S(2)}) collective-permute-start(f32[16,18,1,128]{3,2,1,0:T(1,128)S(1)} %get-tuple-element.14), channel_id=1, source_target_pairs={{0,1},{1,2},{2,3},{3,4},{4,5},{5,6},{6,7},{8,9},{9,10},{10,11},{11... | collective-permute-start | bytes 442376 | tf_op jit(solution)/shard_map/ppermute | solution.py:20
  117.7 11.0 %collective-permute-start.11 = (f32[16,18,1,128]{3,2,1,0:T(1,128)S(1)}, f32[16,18,1,128]{3,2,1,0:T(1,128)S(1)}, u32[]{:S(2)}, u32[]{:S(2)}) collective-permute-start(f32[16,18,1,128]{3,2,1,0:T(1,128)S(1)} %get-tuple-element.15), channel_id=1, source_target_pairs={{1,0},{2,1},{3,2},{4,3},{5,4},{6,5},{7,6},{9,8},{10,9},{11,10},{12... | collective-permute-start | bytes 442376 | tf_op jit(solution)/shard_map/ppermute | solution.py:21
  147.0 14.3 %collective-permute-start.12 = (f32[16,1,32,128]{3,2,1,0:T(8,128)S(1)}, f32[16,1,32,128]{3,2,1,0:T(8,128)S(1)}, u32[]{:S(2)}, u32[]{:S(2)}) collective-permute-start(f32[16,1,32,128]{3,2,1,0:T(8,128)S(1)} %get-tuple-element.20), channel_id=1, source_target_pairs={{0,8},{8,16},{16,24},{24,32},{32,40},{40,48},{48,56},{56,64},{64,7... | collective-permute-start | bytes 786440 | tf_op jit(solution)/shard_map/ppermute | solution.py:20
  150.8 10.5 %collective-permute-start.13 = (f32[16,1,32,128]{3,2,1,0:T(8,128)S(1)}, f32[16,1,32,128]{3,2,1,0:T(8,128)S(1)}, u32[]{:S(2)}, u32[]{:S(2)}) collective-permute-start(f32[16,1,32,128]{3,2,1,0:T(8,128)S(1)} %get-tuple-element.21), channel_id=1, source_target_pairs={{8,0},{16,8},{24,16},{32,24},{40,32},{48,40},{56,48},{64,56},{72,6... | collective-permute-start | bytes 786440 | tf_op jit(solution)/shard_map/ppermute | solution.py:21
  161.5 14.7 %collective-permute-start.14 = (f32[16,18,1,128]{3,2,1,0:T(1,128)S(1)}, f32[16,18,1,128]{3,2,1,0:T(1,128)S(1)}, u32[]{:S(2)}, u32[]{:S(2)}) collective-permute-start(f32[16,18,1,128]{3,2,1,0:T(1,128)S(1)} %get-tuple-element.12), channel_id=1, source_target_pairs={{0,1},{1,2},{2,3},{3,4},{4,5},{5,6},{6,7},{8,9},{9,10},{10,11},{11... | collective-permute-start | bytes 442376 | tf_op jit(solution)/shard_map/ppermute | solution.py:20
  165.5 10.7 %collective-permute-start.15 = (f32[16,18,1,128]{3,2,1,0:T(1,128)S(1)}, f32[16,18,1,128]{3,2,1,0:T(1,128)S(1)}, u32[]{:S(2)}, u32[]{:S(2)}) collective-permute-start(f32[16,18,1,128]{3,2,1,0:T(1,128)S(1)} %get-tuple-element.13), channel_id=1, source_target_pairs={{1,0},{2,1},{3,2},{4,3},{5,4},{6,5},{7,6},{9,8},{10,9},{11,10},{12... | collective-permute-start | bytes 442376 | tf_op jit(solution)/shard_map/ppermute | solution.py:21
  200.5 108.7 %copy-start.14 = (f32[80,64]{1,0:T(8,128)S(1)}, f32[80,64]{1,0:T(8,128)}, u32[]{:S(2)}) copy-start(f32[80,64]{1,0:T(8,128)} %constant.62.clone) | copy-start | bytes 61444
  338.9 17.9 %copy-start.1 = (f32[16,64]{1,0:T(8,128)S(1)}, f32[16,64]{1,0:T(8,128)}, u32[]{:S(2)}) copy-start(f32[16,64]{1,0:T(8,128)} %param.10) | copy-start | bytes 12292
  (10 other events, 46.9 us)
where the time goes:
time: 364 us; the launch traced here: 357 us
  other arithmetic  91.4 us (25%)
  blocking collectives  85.6 us (24%)
  matrix products  58.2 us (16%)
  starting transfers between devices  47.6 us (13%)
  local copies, waits for them, and re-layouts  43.6 us (12%)
  waiting for transfers between devices  29.4 us (8%)
    psum x1, blocking collectives, shards(): gram = lax.psum(jnp.dot(flat, flat.T, precision=highest), ('gx', 'gy'))  85.6 us
    select_n x4, other arithmetic, neighbour_mean(): jnp.where(inside[None], summed / jnp.where(inside, weights, 1.0)[None], 0.0)  38.9 us
    unnamed x45, local copies, waits for them, and re-layouts  37.6 us
    concatenate x4, other arithmetic, with_halo(): value = jnp.concatenate([before, value, after], axis=dim)  36.4 us
    ppermute x8, starting transfers between devices, with_halo(): before = lax.ppermute(last, axis, up)  33.9 us
    dot_general x1, matrix products, shards(): gram = lax.psum(jnp.dot(flat, flat.T, precision=highest), ('gx', 'gy'))  23 us
    ppermute x8, waiting for transfers between devices, with_halo(): after = lax.ppermute(initial, axis, down)  21.1 us
    ppermute x8, starting transfers between devices, with_halo(): after = lax.ppermute(initial, axis, down)  13.8 us
  transfers between devices with their start and end apart: 16, of which 9 were waited for; matrix products, arithmetic and copies ran while one was open for 7% of the time, Pallas kernels for 0%

commit v1 on v0

--- a/solution.py
+++ b/solution.py
@@ -87,7 +87,8 @@
         current = neighbour_mean(padded, conduct_wide)
         krylov.append(current)
     flat = jnp.concatenate([field.reshape(NRHS, -1) for field in krylov], 0)
-    gram = lax.psum(jnp.dot(flat, flat.T, precision=highest), ("gx", "gy"))
+    one_axis = lax.psum(jnp.dot(flat, flat.T, precision=highest), "gy")
+    gram = lax.psum(one_axis, "gx")
     diff, coeffs = least_squares(gram)
     solution = jnp.dot(coeffs.T, flat[: S * NRHS], precision=highest)
     combined = jnp.dot(diff, coeffs, precision=highest)

time: 364 us -> 450 us (1.24)
  the two profiles are of different devices: /device:TPU:1 before, /device:TPU:128 now
where the time goes in v1:
time: 450 us; the launch traced here: 443 us
  blocking collectives  168 us (37%)
  other arithmetic  91.4 us (20%)
  starting transfers between devices  59.6 us (13%)
  matrix products  58.2 us (13%)
  local copies, waits for them, and re-layouts  43.5 us (10%)
  waiting for transfers between devices  21 us (5%)
    psum x1, blocking collectives, shards(): gram = lax.psum(one_axis, 'gx')  140 us
    select_n x4, other arithmetic, neighbour_mean(): jnp.where(inside[None], summed / jnp.where(inside, weights, 1.0)[None], 0.0)  39 us
    unnamed x45, local copies, waits for them, and re-layouts  37.6 us
    concatenate x4, other arithmetic, with_halo(): value = jnp.concatenate([before, value, after], axis=dim)  36.4 us
    ppermute x8, starting transfers between devices, with_halo(): after = lax.ppermute(initial, axis, down)  34.6 us
    psum x1, blocking collectives, shards(): one_axis = lax.psum(jnp.dot(flat, flat.T, precision=highest), 'gy')  27.4 us
    ppermute x8, starting transfers between devices, with_halo(): before = lax.ppermute(last, axis, up)  25 us
    dot_general x1, matrix products, shards(): one_axis = lax.psum(jnp.dot(flat, flat.T, precision=highest), 'gy')  23 us
  transfers between devices with their start and end apart: 16, of which 8 were waited for; matrix products, arithmetic and copies ran while one was open for 6% of the time, Pallas kernels for 0%

profile of v1, /device:TPU:128, one launch (start us, length us, event | category | flops | bytes accessed | tf_op | source)
XLA Modules:
  0.0 442.5 jit_solution(17588083081270935633)
XLA Ops:
  2.0 7.5 %constant_dynamic-update-slice_fusion.3 = (f32[80,65536]{1,0:T(8,128)}, f32[65536,16]{0,1:T(8,128)S(1)}) fusion(f32[65536]{0:T(1024)} %bitcast.93, f32[16,64]{1,0:T(8,128)S(1)} %copy-done, s32[65536]{0:T(1024)} %bitcast.94), kind=kOutput, calls=%fused_computation.175 | convolution fusion | flops 810549248 | bytes 8916992 | tf_op jit(solution)/shard_map/dot_general | solution.py:77
  16.9 5.8 %collective-permute-start.1 = (f32[17,1,32,128]{3,2,1,0:T(8,128)S(1)}, f32[17,1,32,128]{3,2,1,0:T(8,128)S(1)}, u32[]{:S(2)}, u32[]{:S(2)}) collective-permute-start(f32[17,1,32,128]{3,2,1,0:T(8,128)S(1)} %get-tuple-element.19), channel_id=1, source_target_pairs={{8,0},{16,8},{24,16},{32,24},{40,32},{48,40},{56,48},{64,56},{72,6... | collective-permute-start | bytes 835592 | tf_op jit(solution)/shard_map/ppermute | solution.py:21
  36.1 9.7 %select_maximum_fusion.12 = f32[16,18,34,130]{3,2,1,0:T(8,128)} fusion(f32[17,18,1,128]{3,2,1,0:T(1,128)S(1)} %collective-permute-done.3, f32[17,18,1,128]{3,2,1,0:T(1,128)S(1)} %collective-permute-done.2, f32[17,1,32,128]{3,2,1,0:T(8,128)S(1)} %collective-permute-done.1, f32[17,1,32,128]{3,2,1,0:T(8,128)S(1)} %collective-permute-done, ...), kind=kLoop, calls=%fused_computation.25 | loop fusion | flops 17821440 | bytes 10418688 | tf_op jit(solution)/shard_map/concatenate | solution.py:22
  45.8 9.0 %fusion.45 = f32[16,16,32,128]{3,2,1,0:T(8,128)S(1)} fusion(f32[16,18,34,130]{3,2,1,0:T(8,128)} %select_maximum_fusion.12, f32[17,18,1,128]{3,2,1,0:T(1,128)} %copy-done.13, f32[17,1,32,128]{3,2,1,0:T(8,128)} %copy-done.9, f32[17,1,32,128]{3,2,1,0:T(8,128)} %copy-done.8, f32[16,16,32,128]{3,2,1,0:T(8,128)S(1)} %bitcast.84, ...), kind=kLoop, calls=%fused_computation.102 | loop fusion | flops 26214400 | bytes 19810304 | tf_op jit(solution)/shard_map/jit(_where)/select_n | solution.py:44
  56.9 7.6 %collective-permute-start.5 = (f32[16,1,32,128]{3,2,1,0:T(8,128)S(1)}, f32[16,1,32,128]{3,2,1,0:T(8,128)S(1)}, u32[]{:S(2)}, u32[]{:S(2)}) collective-permute-start(f32[16,1,32,128]{3,2,1,0:T(8,128)S(1)} %get-tuple-element.25), channel_id=1, source_target_pairs={{8,0},{16,8},{24,16},{32,24},{40,32},{48,40},{56,48},{64,56},{72,6... | collective-permute-start | bytes 786440 | tf_op jit(solution)/shard_map/ppermute | solution.py:21
  68.6 4.8 %collective-permute-start.6 = (f32[16,18,1,128]{3,2,1,0:T(1,128)S(1)}, f32[16,18,1,128]{3,2,1,0:T(1,128)S(1)}, u32[]{:S(2)}, u32[]{:S(2)}) collective-permute-start(f32[16,18,1,128]{3,2,1,0:T(1,128)S(1)} %get-tuple-element.16), channel_id=1, source_target_pairs={{0,1},{1,2},{2,3},{3,4},{4,5},{5,6},{6,7},{8,9},{9,10},{10,11},{11... | collective-permute-start | bytes 442376 | tf_op jit(solution)/shard_map/ppermute | solution.py:20
  79.0 8.9 %select_maximum_fusion.8 = f32[16,18,34,130]{3,2,1,0:T(8,128)} fusion(f32[16,18,1,128]{3,2,1,0:T(1,128)S(1)} %collective-permute-done.7, f32[16,18,1,128]{3,2,1,0:T(1,128)S(1)} %collective-permute-done.6, f32[16,1,32,128]{3,2,1,0:T(8,128)S(1)} %collective-permute-done.5, f32[16,16,32,128]{3,2,1,0:T(8,128)S(1)} %fusion.45, ...), kind=kLoop, calls=%fused_computation.21 | loop fusion | flops 15275520 | bytes 10105344 | tf_op jit(solution)/shard_map/concatenate | solution.py:22
  87.9 10.9 %fusion.34 = f32[16,16,32,128]{3,2,1,0:T(8,128)S(1)} fusion(f32[16,18,34,130]{3,2,1,0:T(8,128)} %select_maximum_fusion.8, f32[16,18,1,128]{3,2,1,0:T(1,128)S(1)} %collective-permute-done.7, f32[16,1,32,128]{3,2,1,0:T(8,128)S(1)} %collective-permute-done.5, f32[16,16,32,128]{3,2,1,0:T(8,128)S(1)} %fusion.45, ...), kind=kLoop, calls=%fused_computation.81 | loop fusion | flops 22020096 | bytes 19496960 | tf_op jit(solution)/shard_map/jit(_where)/select_n | solution.py:44
  100.7 7.7 %collective-permute-start.9 = (f32[16,1,32,128]{3,2,1,0:T(8,128)S(1)}, f32[16,1,32,128]{3,2,1,0:T(8,128)S(1)}, u32[]{:S(2)}, u32[]{:S(2)}) collective-permute-start(f32[16,1,32,128]{3,2,1,0:T(8,128)S(1)} %get-tuple-element.23), channel_id=1, source_target_pairs={{8,0},{16,8},{24,16},{32,24},{40,32},{48,40},{56,48},{64,56},{72,6... | collective-permute-start | bytes 786440 | tf_op jit(solution)/shard_map/ppermute | solution.py:21
  112.5 4.8 %collective-permute-start.10 = (f32[16,18,1,128]{3,2,1,0:T(1,128)S(1)}, f32[16,18,1,128]{3,2,1,0:T(1,128)S(1)}, u32[]{:S(2)}, u32[]{:S(2)}) collective-permute-start(f32[16,18,1,128]{3,2,1,0:T(1,128)S(1)} %get-tuple-element.14), channel_id=1, source_target_pairs={{0,1},{1,2},{2,3},{3,4},{4,5},{5,6},{6,7},{8,9},{9,10},{10,11},{11... | collective-permute-start | bytes 442376 | tf_op jit(solution)/shard_map/ppermute | solution.py:20
  129.0 8.9 %select_maximum_fusion.4 = f32[16,18,34,130]{3,2,1,0:T(8,128)} fusion(f32[16,18,1,128]{3,2,1,0:T(1,128)S(1)} %collective-permute-done.11, f32[16,18,1,128]{3,2,1,0:T(1,128)S(1)} %collective-permute-done.10, f32[16,1,32,128]{3,2,1,0:T(8,128)S(1)} %collective-permute-done.9, f32[16,16,32,128]{3,2,1,0:T(8,128)S(1)} %fusion.34, ...), kind=kLoop, calls=%fused_computation.17 | loop fusion | flops 15275520 | bytes 10105344 | tf_op jit(solution)/shard_map/concatenate | solution.py:22
  137.9 8.2 %fusion.23 = f32[16,16,32,128]{3,2,1,0:T(8,128)S(1)} fusion(f32[16,18,34,130]{3,2,1,0:T(8,128)} %select_maximum_fusion.4, f32[16,18,1,128]{3,2,1,0:T(1,128)} %copy-done.16, f32[16,1,32,128]{3,2,1,0:T(8,128)} %copy-done.11, f32[16,16,32,128]{3,2,1,0:T(8,128)S(1)} %fusion.34, f32[16,1,32,128]{3,2,1,0:T(8,128)} %copy-done.10, f32[16,18,1,128]{3,2,1,0:T(1,128)} %copy-done.15, ...), kind=kLoop, calls=%fused_computation.60 | loop fusion | flops 22020096 | bytes 19496960 | tf_op jit(solution)/shard_map/jit(_where)/select_n | solution.py:44
  148.0 7.8 %collective-permute-start.13 = (f32[16,1,32,128]{3,2,1,0:T(8,128)S(1)}, f32[16,1,32,128]{3,2,1,0:T(8,128)S(1)}, u32[]{:S(2)}, u32[]{:S(2)}) collective-permute-start(f32[16,1,32,128]{3,2,1,0:T(8,128)S(1)} %get-tuple-element.21), channel_id=1, source_target_pairs={{8,0},{16,8},{24,16},{32,24},{40,32},{48,40},{56,48},{64,56},{72,6... | collective-permute-start | bytes 786440 | tf_op jit(solution)/shard_map/ppermute | solution.py:21
  164.9 4.8 %collective-permute-start.14 = (f32[16,18,1,128]{3,2,1,0:T(1,128)S(1)}, f32[16,18,1,128]{3,2,1,0:T(1,128)S(1)}, u32[]{:S(2)}, u32[]{:S(2)}) collective-permute-start(f32[16,18,1,128]{3,2,1,0:T(1,128)S(1)} %get-tuple-element.12), channel_id=1, source_target_pairs={{0,1},{1,2},{2,3},{3,4},{4,5},{5,6},{6,7},{8,9},{9,10},{10,11},{11... | collective-permute-start | bytes 442376 | tf_op jit(solution)/shard_map/ppermute | solution.py:20
  179.8 9.0 %select_maximum_fusion = f32[16,18,34,130]{3,2,1,0:T(8,128)} fusion(f32[16,18,1,128]{3,2,1,0:T(1,128)S(1)} %collective-permute-done.15, f32[16,18,1,128]{3,2,1,0:T(1,128)S(1)} %collective-permute-done.14, f32[16,1,32,128]{3,2,1,0:T(8,128)S(1)} %collective-permute-done.13, f32[16,16,32,128]{3,2,1,0:T(8,128)S(1)} %fusion.23, ...), kind=kLoop, calls=%fused_computation.13 | loop fusion | flops 15275520 | bytes 10105344 | tf_op jit(solution)/shard_map/concatenate | solution.py:22
  188.8 10.9 %fusion.12 = f32[16,16,32,128]{3,2,1,0:T(8,128)S(1)} fusion(f32[16,18,34,130]{3,2,1,0:T(8,128)} %select_maximum_fusion, f32[16,18,1,128]{3,2,1,0:T(1,128)S(1)} %collective-permute-done.15, f32[16,1,32,128]{3,2,1,0:T(8,128)S(1)} %collective-permute-done.13, f32[16,16,32,128]{3,2,1,0:T(8,128)S(1)} %fusion.23, ...), kind=kLoop, calls=%fused_computation.39 | loop fusion | flops 22020096 | bytes 19496960 | tf_op jit(solution)/shard_map/jit(_where)/select_n | solution.py:44
  204.1 23.0 %fusion.85 = f32[80,80]{1,0:T(8,128)S(1)} fusion(f32[80,65536]{1,0:T(8,128)} %bitcast_dynamic-update-slice_fusion), kind=kOutput, calls=%fused_computation.182 | convolution fusion | flops 5033164800 | bytes 20997120 | tf_op jit(solution)/shard_map/dot_general | solution.py:90
  227.1 27.4 %psum.14 = f32[80,80]{1,0:T(8,128)S(1)} all-reduce(f32[80,80]{1,0:T(8,128)S(1)} %fusion.85), channel_id=1, replica_groups=mesh['gx'=32,'gy'=8] {'gy'}, use_global_device_ids=true, to_apply=%region_0.1 | all-reduce | flops 6400 | bytes 51200 | tf_op jit(solution)/shard_map/psum | solution.py:90
  254.4 140.2 %psum.15 = f32[80,80]{1,0:T(8,128)S(1)} all-reduce(f32[80,80]{1,0:T(8,128)S(1)} %psum.14), channel_id=1, replica_groups=mesh['gx'=32,'gy'=8] {'gx'}, use_global_device_ids=true, to_apply=%region_1.2 | all-reduce | flops 6400 | bytes 51200 | tf_op jit(solution)/shard_map/psum | solution.py:91
  395.4 5.8 %cholesky.16 = f32[64,64]{1,0:T(8,128)S(1)} custom-call(f32[64,64]{1,0:T(8,128)S(1)} %fusion.73), custom_call_target="Cholesky" | custom-call | tf_op jit(solution)/shard_map/jit(cholesky)/cholesky | solution.py:61
  402.6 4.9 %custom-call.10 = f32[1,64,64]{1,2,0:T(8,128)S(1)} custom-call(f32[1,64,64]{2,1,0:T(8,128)S(1)} %fusion.68), custom_call_target="InvertDiagBlocksLowerTriangular" | custom-call | tf_op jit(solution)/shard_map/jit(_cho_solve)/triangular_solve | solution.py:62
  408.1 13.5 %fusion.57 = f32[2,8,512,128]{3,1,2,0:T(8,128)S(1)} fusion(f32[16,80]{1,0:T(8,128)S(1)} %fusion.88, f32[80,65536]{1,0:T(8,128)} %bitcast_dynamic-update-slice_fusion, f32[65536,16]{0,1:T(8,128)} %copy-done.2), kind=kOutput, calls=%fused_computation.125 | convolution fusion | flops 1007681536 | bytes 29365248 | tf_op jit(solution)/shard_map/dot_general | solution.py:95
  424.4 12.9 %fusion.54 = f32[2,8,512,128]{3,1,2,0:T(8,128)} fusion(f32[64,16]{0,1:T(8,128)S(1)} %fusion.69, f32[16,65536]{1,0:T(8,128)} %bitcast.90, f32[16,65536]{1,0:T(8,128)} %bitcast.89, f32[16,65536]{1,0:T(8,128)} %bitcast.88, f32[16,65536]{1,0:T(8,128)} %bitcast.86), kind=kOutput, calls=%fused_computation.124 | convolution fusion | flops 817889280 | bytes 20975616 | tf_op jit(solution)/shard_map/dot_general | solution.py:93
  437.3 5.0 %copy.14 = f32[2,8,512,128]{3,2,1,0:T(8,128)} copy(f32[2,8,512,128]{3,1,2,0:T(8,128)} %fusion.54) | data formatting | bytes 8388608
  (93 shorter events, 82.4 us)
Async XLA Ops:
  13.5 13.6 %collective-permute-start = (f32[17,1,32,128]{3,2,1,0:T(8,128)S(1)}, f32[17,1,32,128]{3,2,1,0:T(8,128)S(1)}, u32[]{:S(2)}, u32[]{:S(2)}) collective-permute-start(f32[17,1,32,128]{3,2,1,0:T(8,128)S(1)} %get-tuple-element.18), channel_id=1, source_target_pairs={{0,8},{8,16},{16,24},{24,32},{32,40},{40,48},{48,56},{56,64},{64,7... | collective-permute-start | bytes 835592 | tf_op jit(solution)/shard_map/ppermute | solution.py:20
  16.9 11.4 %collective-permute-start.1 = (f32[17,1,32,128]{3,2,1,0:T(8,128)S(1)}, f32[17,1,32,128]{3,2,1,0:T(8,128)S(1)}, u32[]{:S(2)}, u32[]{:S(2)}) collective-permute-start(f32[17,1,32,128]{3,2,1,0:T(8,128)S(1)} %get-tuple-element.19), channel_id=1, source_target_pairs={{8,0},{16,8},{24,16},{32,24},{40,32},{48,40},{56,48},{64,56},{72,6... | collective-permute-start | bytes 835592 | tf_op jit(solution)/shard_map/ppermute | solution.py:21
  28.5 2.6 collective-permute-start.2
  29.8 5.1 %collective-permute-start.3 = (f32[17,18,1,128]{3,2,1,0:T(1,128)S(1)}, f32[17,18,1,128]{3,2,1,0:T(1,128)S(1)}, u32[]{:S(2)}, u32[]{:S(2)}) collective-permute-start(f32[17,18,1,128]{3,2,1,0:T(1,128)S(1)} %get-tuple-element.11), channel_id=1, source_target_pairs={{1,0},{2,1},{3,2},{4,3},{5,4},{6,5},{7,6},{9,8},{10,9},{11,10},{12... | collective-permute-start | bytes 470024 | tf_op jit(solution)/shard_map/ppermute | solution.py:21
  54.9 12.1 %collective-permute-start.4 = (f32[16,1,32,128]{3,2,1,0:T(8,128)S(1)}, f32[16,1,32,128]{3,2,1,0:T(8,128)S(1)}, u32[]{:S(2)}, u32[]{:S(2)}) collective-permute-start(f32[16,1,32,128]{3,2,1,0:T(8,128)S(1)} %get-tuple-element.24), channel_id=1, source_target_pairs={{0,8},{8,16},{16,24},{24,32},{32,40},{40,48},{48,56},{56,64},{64,7... | collective-permute-start | bytes 786440 | tf_op jit(solution)/shard_map/ppermute | solution.py:20
  56.9 11.5 %collective-permute-start.5 = (f32[16,1,32,128]{3,2,1,0:T(8,128)S(1)}, f32[16,1,32,128]{3,2,1,0:T(8,128)S(1)}, u32[]{:S(2)}, u32[]{:S(2)}) collective-permute-start(f32[16,1,32,128]{3,2,1,0:T(8,128)S(1)} %get-tuple-element.25), channel_id=1, source_target_pairs={{8,0},{16,8},{24,16},{32,24},{40,32},{48,40},{56,48},{64,56},{72,6... | collective-permute-start | bytes 786440 | tf_op jit(solution)/shard_map/ppermute | solution.py:21
  68.6 6.5 %collective-permute-start.6 = (f32[16,18,1,128]{3,2,1,0:T(1,128)S(1)}, f32[16,18,1,128]{3,2,1,0:T(1,128)S(1)}, u32[]{:S(2)}, u32[]{:S(2)}) collective-permute-start(f32[16,18,1,128]{3,2,1,0:T(1,128)S(1)} %get-tuple-element.16), channel_id=1, source_target_pairs={{0,1},{1,2},{2,3},{3,4},{4,5},{5,6},{6,7},{8,9},{9,10},{10,11},{11... | collective-permute-start | bytes 442376 | tf_op jit(solution)/shard_map/ppermute | solution.py:20
  73.4 14.4 %copy-start.3 = (f32[16,32,128]{2,1,0:T(8,128)S(1)}, f32[16,32,128]{2,1,0:T(8,128)}, u32[]{:S(2)}) copy-start(f32[16,32,128]{2,1,0:T(8,128)} %get-tuple-element.6) | copy-start | bytes 786436
  73.4 14.4 %copy-start.4 = (f32[16,32,128]{2,1,0:T(8,128)S(1)}, f32[16,32,128]{2,1,0:T(8,128)}, u32[]{:S(2)}) copy-start(f32[16,32,128]{2,1,0:T(8,128)} %get-tuple-element.7) | copy-start | bytes 786436
  73.5 14.4 %copy-start.6 = (f32[16,32,128]{2,1,0:T(8,128)S(1)}, f32[16,32,128]{2,1,0:T(8,128)}, u32[]{:S(2)}) copy-start(f32[16,32,128]{2,1,0:T(8,128)} %get-tuple-element.8) | copy-start | bytes 786436
  73.5 5.5 %collective-permute-start.7 = (f32[16,18,1,128]{3,2,1,0:T(1,128)S(1)}, f32[16,18,1,128]{3,2,1,0:T(1,128)S(1)}, u32[]{:S(2)}, u32[]{:S(2)}) collective-permute-start(f32[16,18,1,128]{3,2,1,0:T(1,128)S(1)} %get-tuple-element.17), channel_id=1, source_target_pairs={{1,0},{2,1},{3,2},{4,3},{5,4},{6,5},{7,6},{9,8},{10,9},{11,10},{12... | collective-permute-start | bytes 442376 | tf_op jit(solution)/shard_map/ppermute | solution.py:21
  98.8 12.1 %collective-permute-start.8 = (f32[16,1,32,128]{3,2,1,0:T(8,128)S(1)}, f32[16,1,32,128]{3,2,1,0:T(8,128)S(1)}, u32[]{:S(2)}, u32[]{:S(2)}) collective-permute-start(f32[16,1,32,128]{3,2,1,0:T(8,128)S(1)} %get-tuple-element.22), channel_id=1, source_target_pairs={{0,8},{8,16},{16,24},{24,32},{32,40},{40,48},{48,56},{56,64},{64,7... | collective-permute-start | bytes 786440 | tf_op jit(solution)/shard_map/ppermute | solution.py:20
  100.7 11.6 %collective-permute-start.9 = (f32[16,1,32,128]{3,2,1,0:T(8,128)S(1)}, f32[16,1,32,128]{3,2,1,0:T(8,128)S(1)}, u32[]{:S(2)}, u32[]{:S(2)}) collective-permute-start(f32[16,1,32,128]{3,2,1,0:T(8,128)S(1)} %get-tuple-element.23), channel_id=1, source_target_pairs={{8,0},{16,8},{24,16},{32,24},{40,32},{48,40},{56,48},{64,56},{72,6... | collective-permute-start | bytes 786440 | tf_op jit(solution)/shard_map/ppermute | solution.py:21
  110.9 16.9 %copy-start.10 = (f32[16,1,32,128]{3,2,1,0:T(8,128)}, f32[16,1,32,128]{3,2,1,0:T(8,128)S(1)}, u32[]{:S(2)}) copy-start(f32[16,1,32,128]{3,2,1,0:T(8,128)S(1)} %collective-permute-done.8) | copy-start | bytes 786436
  112.3 15.4 %copy-start.11 = (f32[16,1,32,128]{3,2,1,0:T(8,128)}, f32[16,1,32,128]{3,2,1,0:T(8,128)S(1)}, u32[]{:S(2)}) copy-start(f32[16,1,32,128]{3,2,1,0:T(8,128)S(1)} %collective-permute-done.9) | copy-start | bytes 786436
  112.5 15.2 %collective-permute-start.10 = (f32[16,18,1,128]{3,2,1,0:T(1,128)S(1)}, f32[16,18,1,128]{3,2,1,0:T(1,128)S(1)}, u32[]{:S(2)}, u32[]{:S(2)}) collective-permute-start(f32[16,18,1,128]{3,2,1,0:T(1,128)S(1)} %get-tuple-element.14), channel_id=1, source_target_pairs={{0,1},{1,2},{2,3},{3,4},{4,5},{5,6},{6,7},{8,9},{9,10},{10,11},{11... | collective-permute-start | bytes 442376 | tf_op jit(solution)/shard_map/ppermute | solution.py:20
  117.4 10.3 %collective-permute-start.11 = (f32[16,18,1,128]{3,2,1,0:T(1,128)S(1)}, f32[16,18,1,128]{3,2,1,0:T(1,128)S(1)}, u32[]{:S(2)}, u32[]{:S(2)}) collective-permute-start(f32[16,18,1,128]{3,2,1,0:T(1,128)S(1)} %get-tuple-element.15), channel_id=1, source_target_pairs={{1,0},{2,1},{3,2},{4,3},{5,4},{6,5},{7,6},{9,8},{10,9},{11,10},{12... | collective-permute-start | bytes 442376 | tf_op jit(solution)/shard_map/ppermute | solution.py:21
  127.7 10.2 %copy-start.7 = (f32[16,32,128]{2,1,0:T(8,128)S(1)}, f32[16,32,128]{2,1,0:T(8,128)}, u32[]{:S(2)}) copy-start(f32[16,32,128]{2,1,0:T(8,128)} %get-tuple-element.8) | copy-start | bytes 786436
  146.1 18.6 %collective-permute-start.12 = (f32[16,1,32,128]{3,2,1,0:T(8,128)S(1)}, f32[16,1,32,128]{3,2,1,0:T(8,128)S(1)}, u32[]{:S(2)}, u32[]{:S(2)}) collective-permute-start(f32[16,1,32,128]{3,2,1,0:T(8,128)S(1)} %get-tuple-element.20), channel_id=1, source_target_pairs={{0,8},{8,16},{16,24},{24,32},{32,40},{40,48},{48,56},{56,64},{64,7... | collective-permute-start | bytes 786440 | tf_op jit(solution)/shard_map/ppermute | solution.py:20
  148.0 16.6 %collective-permute-start.13 = (f32[16,1,32,128]{3,2,1,0:T(8,128)S(1)}, f32[16,1,32,128]{3,2,1,0:T(8,128)S(1)}, u32[]{:S(2)}, u32[]{:S(2)}) collective-permute-start(f32[16,1,32,128]{3,2,1,0:T(8,128)S(1)} %get-tuple-element.21), channel_id=1, source_target_pairs={{8,0},{16,8},{24,16},{32,24},{40,32},{48,40},{56,48},{64,56},{72,6... | collective-permute-start | bytes 786440 | tf_op jit(solution)/shard_map/ppermute | solution.py:21
  164.9 14.9 %collective-permute-start.14 = (f32[16,18,1,128]{3,2,1,0:T(1,128)S(1)}, f32[16,18,1,128]{3,2,1,0:T(1,128)S(1)}, u32[]{:S(2)}, u32[]{:S(2)}) collective-permute-start(f32[16,18,1,128]{3,2,1,0:T(1,128)S(1)} %get-tuple-element.12), channel_id=1, source_target_pairs={{0,1},{1,2},{2,3},{3,4},{4,5},{5,6},{6,7},{8,9},{9,10},{10,11},{11... | collective-permute-start | bytes 442376 | tf_op jit(solution)/shard_map/ppermute | solution.py:20
  169.6 10.1 %collective-permute-start.15 = (f32[16,18,1,128]{3,2,1,0:T(1,128)S(1)}, f32[16,18,1,128]{3,2,1,0:T(1,128)S(1)}, u32[]{:S(2)}, u32[]{:S(2)}) collective-permute-start(f32[16,18,1,128]{3,2,1,0:T(1,128)S(1)} %get-tuple-element.13), channel_id=1, source_target_pairs={{1,0},{2,1},{3,2},{4,3},{5,4},{6,5},{7,6},{9,8},{10,9},{11,10},{12... | collective-permute-start | bytes 442376 | tf_op jit(solution)/shard_map/ppermute | solution.py:21
  204.1 190.6 %copy-start.14 = (f32[80,64]{1,0:T(8,128)S(1)}, f32[80,64]{1,0:T(8,128)}, u32[]{:S(2)}) copy-start(f32[80,64]{1,0:T(8,128)} %constant.62.clone) | copy-start | bytes 61444
  424.4 17.9 %copy-start.1 = (f32[16,64]{1,0:T(8,128)S(1)}, f32[16,64]{1,0:T(8,128)}, u32[]{:S(2)}) copy-start(f32[16,64]{1,0:T(8,128)} %param.10) | copy-start | bytes 12292
  (10 other events, 39.9 us)
